TPU v7x, 32 devices: a whole 2x2x4 slice. The times are simulated.
32 devices in a mesh: ax: 4 (over x, core), circ: 8 (over z, y).
Axes of the slice: x: 2, y: 2, z: 4, core: 2. Of those that a mesh axis runs over, the one named last changes fastest.
Arguments:
- load: float32 [32, 256, 3, 192], P('ax', 'circ'), may hold values from -6 to 6
- region: int32 [32, 256, 192], P('ax', 'circ'), may hold values from 0 to 1
- family: int32 [32, 256, 192], P('ax', 'circ'), may hold values from 0 to 1, as said below
- stiffness: float32 [2, 3], replicated, may hold values from 1 to 4
- coupling: float32 [2, 3, 3], replicated, may hold values from -0.6 to 0.6
- line_inverse: float32 [3, 3, 192, 192], replicated, may hold values from 0 to 1
- axial_inverse: float32 [8, 8], replicated, may hold values from 0 to 2
Outputs:
- solution: float32 [32, 256, 3, 192], P('ax', 'circ')
- residual: float32 [32, 256, 3, 192], P('ax', 'circ')
- coarse_iterate: float32 [8, 256, 3, 192], P('ax', 'circ')
Inputs may be any that keep to these rules, and one draw needn't show every extreme that they name: family is 0 or 1 per cell.
All inputs are finite; a program needn't handle non-finite values.
Results may differ from a plain program's by a relative error of at most 0.0003.
Values sent between devices are 32-bit elements; how exact they have to be, the bound alone decides.
A program may use at most 128 MiB of HBM per device.

v0:
```python
import functools

import jax
import jax.numpy as jnp
from jax import lax
from jax.experimental import pallas as pl
from jax.experimental.pallas import tpu as pltpu
from jax.sharding import PartitionSpec as P

RADIAL_WEIGHT = 1024.0
DAMPING = 0.8
F32 = jnp.float32
BF16 = jnp.bfloat16
DEEP = 4


def kernel(
    dims,
    load_ref,
    region_ref,
    family_ref,
    stiff_ref,
    coup_ref,
    inv_ref,
    axial_ref,
    sol_ref,
    res_ref,
    coarse_ref,
    b0,
    u0a,
    u0b,
    u0c,
    u0d,
    u0e,
    b1,
    u1a,
    u1b,
    u1c,
    u1d,
    u1e,
    b2,
    c2,
    u2,
    y2,
    rbuf,
    reg0,
    sh0,
    reg1,
    sh1,
    ends0,
    ends1,
    wh,
    wm,
    wl,
    wtmp,
    pack0,
    got0,
    pack1,
    got1,
    packc,
    gotc,
    packb,
    gotb,
    send_sem,
    recv_sem,
    gsend,
    grecv,
    csend,
    crecv,
):
    nax, ncirc, ca, cc, rr, lanes = dims
    ce = cc + 2 * DEEP
    cm, cq = ca // 2, ca // 4
    na2 = cq * nax
    pos = lax.axis_index("ax")
    me_c = lax.axis_index("circ")
    ax_left, ax_right = lax.rem(pos + nax - 1, nax), lax.rem(pos + 1, nax)
    c_left, c_right = lax.rem(me_c + ncirc - 1, ncirc), lax.rem(me_c + 1, ncirc)
    has_left, has_right = pos > 0, pos < nax - 1

    barrier = pltpu.get_barrier_semaphore()
    for d in range(1, nax):
        pl.semaphore_signal(barrier, inc=1, device_id=(lax.rem(pos + d, nax), me_c))
    pl.semaphore_signal(barrier, inc=1, device_id=(pos, c_left))
    pl.semaphore_signal(barrier, inc=1, device_id=(pos, c_right))

    b0[:, 1 : ca + 1, 0:cc, lanes - 128 : lanes] = jnp.zeros((3, ca, cc, 128), F32)
    for k in range(3):
        b0[k, 1 : ca + 1, 0:cc, 0:rr] = load_ref[:, k]

    def zero_row(buf, row):
        buf[:, row] = jnp.zeros((3, ce, lanes), F32)

    @pl.when(jnp.logical_not(has_left))
    def _():
        for buf in (b0, u0b, u1a, u1b, u1d, u1e, u0d, u0e):
            zero_row(buf, 0)

    @pl.when(jnp.logical_not(has_right))
    def _():
        for buf, row in (
            (b0, ca + 1),
            (u0b, ca + 1),
            (u0d, ca + 1),
            (u0e, ca + 1),
            (u1a, cm + 1),
            (u1b, cm + 1),
            (u1d, cm + 1),
            (u1e, cm + 1),
        ):
            zero_row(buf, row)

    zero_row(u2, 0)
    zero_row(u2, na2 + 1)

    def edge_copies(x, buf, rows, pack, got):
        left = pltpu.make_async_remote_copy(
            src_ref=buf.at[:, 1, 0:cc],
            dst_ref=buf.at[:, rows + 1, 0:cc],
            send_sem=send_sem.at[x, 0],
            recv_sem=recv_sem.at[x, 1],
            device_id=(ax_left, me_c),
        )
        right = pltpu.make_async_remote_copy(
            src_ref=buf.at[:, rows, 0:cc],
            dst_ref=buf.at[:, 0, 0:cc],
            send_sem=send_sem.at[x, 1],
            recv_sem=recv_sem.at[x, 0],
            device_id=(ax_right, me_c),
        )
        down = pltpu.make_async_remote_copy(
            src_ref=pack.at[0],
            dst_ref=got.at[0],
            send_sem=send_sem.at[x, 2],
            recv_sem=recv_sem.at[x, 2],
            device_id=(pos, c_left),
        )
        up = pltpu.make_async_remote_copy(
            src_ref=pack.at[1],
            dst_ref=got.at[1],
            send_sem=send_sem.at[x, 3],
            recv_sem=recv_sem.at[x, 3],
            device_id=(pos, c_right),
        )
        return left, right, down, up

    def edge_start(x, buf, rows, pack, got):
        left, right, down, up = edge_copies(x, buf, rows, pack, got)
        for k in range(3):
            for a in range(rows):
                pack[0, k * rows + a : k * rows + a + 1, :] = buf[k, a + 1, 0:1, :]
                pack[1, k * rows + a : k * rows + a + 1, :] = buf[k, a + 1, cc - 1 : cc, :]
        down.start()
        up.start()

        @pl.when(has_left)
        def _():
            left.start()

        @pl.when(has_right)
        def _():
            right.start()

    def edge_finish(x, buf, rows, pack, got, keep=False):
        left, right, down, up = edge_copies(x, buf, rows, pack, got)
        down.wait()
        up.wait()
        for k in range(3 if keep else 0):
            for a in range(rows):
                buf[k, a + 1, cc : cc + 1, :] = got[0, k * rows + a : k * rows + a + 1, :]
                buf[k, a + 1, ce - 1 : ce, :] = got[1, k * rows + a : k * rows + a + 1, :]

        @pl.when(has_left)
        def _():
            left.wait_send()
            right.wait_recv()

        @pl.when(has_right)
        def _():
            right.wait_send()
            left.wait_recv()

    def gather_copies(which, buf):
        pairs = []
        for d in range(1, nax):
            to, of = lax.rem(pos + d, nax), lax.rem(pos + nax - d, nax)
            out = pltpu.make_async_remote_copy(
                src_ref=buf.at[:, pl.ds(pos * cq, cq), 0:cc],
                dst_ref=buf.at[:, pl.ds(pos * cq, cq), 0:cc],
                send_sem=gsend.at[which, d],
                recv_sem=grecv.at[which, d],
                device_id=(to, me_c),
            )
            come = pltpu.make_async_remote_copy(
                src_ref=buf.at[:, pl.ds(of * cq, cq), 0:cc],
                dst_ref=buf.at[:, pl.ds(of * cq, cq), 0:cc],
                send_sem=gsend.at[which, d],
                recv_sem=grecv.at[which, d],
                device_id=(to, me_c),
            )
            pairs.append((out, come))
        return pairs

    half = na2 // 2
    low = lax.broadcasted_iota(jnp.int32, (8, lanes), 0) < DEEP

    def turn(tile):
        return pltpu.roll(tile, DEEP, 0)

    def deep_copies(which, pack, got):
        return [
            pltpu.make_async_remote_copy(
                src_ref=pack.at[side],
                dst_ref=got.at[side],
                send_sem=csend.at[which, side],
                recv_sem=crecv.at[which, side],
                device_id=(pos, (c_left, c_right)[side]),
            )
            for side in range(2)
        ]

    def deep_start(which, buf, fields, pack, got):
        for f in range(fields):
            for a in range(half):
                pack[0, f, a] = jnp.where(low, buf[f, a, 0:8, :], turn(buf[f, a + half, 0:8, :]))
                pack[1, f, a] = jnp.where(
                    low, turn(buf[f, a, cc - 8 : cc, :]), buf[f, a + half, cc - 8 : cc, :]
                )
        for copy in deep_copies(which, pack, got):
            copy.start()

    def deep_finish(which, buf, fields, pack, got):
        for copy in deep_copies(which, pack, got):
            copy.wait()
        for f in range(fields):
            for a in range(half):
                right, left = got[0, f, a], got[1, f, a]
                buf[f, a, cc:ce, :] = jnp.where(low, right, turn(left))
                buf[f, a + half, cc:ce, :] = jnp.where(low, turn(right), left)

    def split(x):
        hi = x.astype(BF16)
        rest = x - hi.astype(F32)
        mid = rest.astype(BF16)
        return hi, mid, (rest - mid.astype(F32)).astype(BF16)

    def line(level, k, x):
        hi, mid, lo = split(x)
        i = level * 3 + k
        dot = functools.partial(jnp.dot, preferred_element_type=F32)
        small = dot(lo, wh[i]) + dot(hi, wl[i]) + dot(mid, wm[i])
        return dot(hi, wh[i]) + (dot(mid, wh[i]) + dot(hi, wm[i]) + small)

    stiff = [[stiff_ref[s, k] for k in range(3)] for s in range(2)]
    first = [[coup_ref[k, 0, e] for e in range(3)] for k in range(3)]
    diff = [[coup_ref[k, 1, e] - first[k][e] for e in range(3)] for k in range(3)]

    coefs = [(reg0, sh0), (reg1, sh1), (c2.at[0], c2.at[1])]
    edges = [ends0, ends1]

    def remainder(u, level, begin, count, stride, cols, rhs, shift, wrap):
        weight, (reg, share) = 0.25**level, coefs[level]
        gain = [stiff[1][k] - stiff[0][k] for k in range(3)]

        def row(step, carry):
            a = begin + step * stride
            own = [u[k, a + 1, 0:cols, :] for k in range(3)]
            region, fibre = reg[a, 0:cols, :], share[a, 0:cols, :]
            for k in range(3):
                c = own[k]
                if wrap:
                    around = pltpu.roll(c, 1, 0) + pltpu.roll(c, cols - 1, 0)
                else:
                    wide = u[k, a + 1]
                    around = pltpu.roll(wide, 1, 0)[0:cols] + pltpu.roll(wide, ce - 1, 0)[0:cols]
                beside = pltpu.roll(c, 1, 1) + pltpu.roll(c, lanes - 1, 1)
                axial = u[k, a, 0:cols, :] + u[k, a + 2, 0:cols, :]
                lap = (
                    (2.0 * weight + 2.0 + 2.0 * RADIAL_WEIGHT) * c
                    - weight * axial
                    - around
                    - RADIAL_WEIGHT * beside
                )
                mix = own[0] * first[k][0] + own[1] * first[k][1] + own[2] * first[k][2]
                more = own[0] * diff[k][0] + own[1] * diff[k][1] + own[2] * diff[k][2]
                value = (stiff[0][k] + region * gain[k]) * lap + (c + mix + fibre * more)
                rbuf[k, pl.ds(pl.multiple_of(a * cols, 8), cols), :] = (
                    rhs[k, a + shift, 0:cols, :] - value
                )
            return carry

        lax.fori_loop(0, count, row, 0)

    def whole_remainder(u, level, rows, rhs):
        remainder(u, level, 0, rows, 1, cc, rhs, 1, False)

    def edge_remainder(x, u, level, rows, rhs, pack, got, keep=False, between=None):
        edge_start(x, u, rows, pack, got)
        remainder(u, level, 1, rows - 2, 1, cc, rhs, 1, True)
        if between is not None:
            between()
        edge_finish(x, u, rows, pack, got, keep)
        remainder(u, level, 0, 2, rows - 1, cc, rhs, 1, True)
        ends = edges[level]
        for k in range(3):
            at = k * rows
            for side, col in ((0, cc - 1), (1, 0)):
                coef = stiff[0][k] + ends[side, 0:rows, :] * (stiff[1][k] - stiff[0][k])
                more = coef * (got[side, at : at + rows, :] - pack[side, at : at + rows, :])
                for a in range(rows):
                    place = a * cc + col
                    rbuf[k, place : place + 1, :] = rbuf[k, place : place + 1, :] + more[a : a + 1]

    def correct(level, rows, old, new):
        def one(k, carry):
            step = line(level, k, rbuf[k, 0 : rows * cc, :]).reshape(rows, cc, lanes)
            new[k, 1 : rows + 1, 0:cc, :] = old[k, 1 : rows + 1, 0:cc, :] + step
            return carry

        lax.fori_loop(0, 3, one, 0)

    def first_sweep(level, rhs, rows, new):
        def one(k, carry):
            step = line(level, k, rhs[k].reshape(rows * ce, lanes))
            new[k] = step.reshape(rows, ce, lanes)
            return carry

        lax.fori_loop(0, 3, one, 0)

    def start_from(level, rhs, rows, new):
        def one(k, carry):
            step = line(level, k, rhs[k, 1 : rows + 1, 0:cc, :].reshape(rows * cc, lanes))
            new[k, 1 : rows + 1, 0:cc, :] = step.reshape(rows, cc, lanes)
            return carry

        lax.fori_loop(0, 3, one, 0)

    def restrict_into(rows, write):
        for k in range(3):
            r = rbuf[k, 0 : rows * cc, :].reshape(rows // 2, 2, cc, lanes)
            write(k, 0.5 * (r[:, 0] + r[:, 1]))

    pl.semaphore_wait(barrier, nax + 1)
    edge_start(0, b0, ca, pack0, got0)

    zeros = jnp.zeros((ca, cc, lanes), F32)
    reg0[...] = zeros
    sh0[...] = zeros
    reg0[:, :, 0:rr] = jnp.where(region_ref[...] == 0, 0.0, 1.0)
    sh0[:, :, 0:rr] = jnp.where(family_ref[...] == 1, 1.0, 0.0)
    for fine_c, mid_c, f in ((reg0, reg1, 0), (sh0, sh1, 1)):
        for a in range(cm):
            mid_c[a] = 0.5 * (fine_c[2 * a] + fine_c[2 * a + 1])
        for a in range(cq):
            c2[f, pos * cq + a, 0:cc, :] = 0.5 * (mid_c[2 * a] + mid_c[2 * a + 1])
    for out, _ in gather_copies(0, c2):
        out.start()
    for ends, reg, rows in ((ends0, reg0, ca), (ends1, reg1, cm)):
        for a in range(rows):
            ends[0, a : a + 1, :] = reg[a, cc - 1 : cc, :]
            ends[1, a : a + 1, :] = reg[a, 0:1, :]

    wtmp[...] = jnp.zeros((lanes, lanes), F32)

    def prepare(i, carry):
        wtmp[0:rr, 0:rr] = inv_ref[i] * DAMPING
        wh[i], wm[i], wl[i] = split(jnp.transpose(wtmp[...]))
        return carry

    lax.fori_loop(0, 9, prepare, 0)

    edge_finish(0, b0, ca, pack0, got0, True)
    first_sweep(0, b0, ca + 2, u0a)
    whole_remainder(u0a, 0, ca, b0)
    correct(0, ca, u0a, u0b)

    def coefficients_on():
        for out, come in gather_copies(0, c2):
            out.wait_send()
            come.wait_recv()
        deep_start(0, c2, 2, packc, gotc)

    edge_remainder(1, u0b, 0, ca, b0, pack0.at[2:4], got0.at[2:4], True, coefficients_on)

    def into_b1(k, value):
        b1[k, 1 : cm + 1, 0:cc, :] = value

    restrict_into(ca, into_b1)

    start_from(1, b1, cm, u1a)
    edge_remainder(2, u1a, 1, cm, b1, pack1, got1)
    correct(1, cm, u1a, u1b)
    edge_remainder(3, u1b, 1, cm, b1, pack1.at[2:4], got1.at[2:4], True)

    def into_b2(k, value):
        b2[k, pl.ds(pos * cq, cq), 0:cc, :] = value

    restrict_into(cm, into_b2)

    for out, _ in gather_copies(1, b2):
        out.start()
    deep_finish(0, c2, 2, packc, gotc)
    for out, come in gather_copies(1, b2):
        out.wait_send()
        come.wait_recv()
    deep_start(1, b2, 3, packb, gotb)
    deep_finish(1, b2, 3, packb, gotb)

    def coarse_solve(first_time):
        def one(k, carry):
            x = b2[k].reshape(na2 * ce, lanes) if first_time else rbuf[k, 0 : na2 * ce, :]
            y2[...] = line(2, k, x).reshape(na2, ce, lanes)

            def row(a, inner):
                total = axial_ref[a, 0] * y2[0]
                for b in range(1, na2):
                    total = total + axial_ref[a, b] * y2[b]
                u2[k, a + 1] = total if first_time else u2[k, a + 1] + total
                return inner

            return lax.fori_loop(0, na2, row, carry)

        lax.fori_loop(0, 3, one, 0)

    coarse_solve(True)

    def coarse_sweep(turn_number, carry):
        remainder(u2, 2, 0, na2, 1, ce, b2, 0, True)
        coarse_solve(False)
        return carry

    lax.fori_loop(0, 3, coarse_sweep, 0)

    for a in range(cq):
        for k in range(3):
            coarse_ref[a, k] = u2[k, pos * cq + a + 1, 0:cc, 0:rr]

    for i in range(cm + 2):
        for k in range(3):
            u1c[k, i] = u1b[k, i] + u2[k, pos * cq + (i + 1) // 2]
    whole_remainder(u1c, 1, cm, b1)
    correct(1, cm, u1c, u1d)
    edge_remainder(4, u1d, 1, cm, b1, pack1.at[4:6], got1.at[4:6])
    correct(1, cm, u1d, u1e)
    edge_start(5, u1e, cm, pack1.at[6:8], got1.at[6:8])
    edge_finish(5, u1e, cm, pack1.at[6:8], got1.at[6:8], True)

    for i in range(ca + 2):
        for k in range(3):
            u0c[k, i] = u0b[k, i] + u1e[k, (i + 1) // 2]
    whole_remainder(u0c, 0, ca, b0)
    correct(0, ca, u0c, u0d)
    edge_remainder(6, u0d, 0, ca, b0, pack0.at[4:6], got0.at[4:6])
    correct(0, ca, u0d, u0e)

    def solution_out():
        for k in range(3):
            sol_ref[:, k] = u0e[k, 1 : ca + 1, 0:cc, 0:rr]

    edge_remainder(7, u0e, 0, ca, b0, pack0.at[6:8], got0.at[6:8], False, solution_out)
    for k in range(3):
        res_ref[:, k] = rbuf[k, 0 : ca * cc, 0:rr].reshape(ca, cc, rr)


def body(load, region, family, stiffness, coupling, line_inverse, axial_inverse):
    nax, ncirc = lax.axis_size("ax"), lax.axis_size("circ")
    ca, cc, _, rr = load.shape
    lanes = -(-rr // 128) * 128
    ce = cc + 2 * DEEP
    cm, cq = ca // 2, ca // 4
    na2 = cq * nax
    rows = max(ca * cc, na2 * ce)
    rows1 = -(-3 * cm // 8) * 8
    vmem = pl.BlockSpec(memory_space=pltpu.VMEM)
    smem = pl.BlockSpec(memory_space=pltpu.SMEM)
    fine = pltpu.VMEM((3, ca + 2, ce, lanes), F32)
    mid = pltpu.VMEM((3, cm + 2, ce, lanes), F32)
    half = na2 // 2
    sol, res, coarse = pl.pallas_call(
        functools.partial(kernel, (nax, ncirc, ca, cc, rr, lanes)),
        out_shape=[
            jax.ShapeDtypeStruct((ca, 3, cc, rr), F32),
            jax.ShapeDtypeStruct((ca, 3, cc, rr), F32),
            jax.ShapeDtypeStruct((cq, 3, cc, rr), F32),
        ],
        in_specs=[vmem, vmem, vmem, smem, smem, vmem, smem],
        out_specs=[vmem, vmem, vmem],
        scratch_shapes=[fine] * 6
        + [mid] * 6
        + [
            pltpu.VMEM((3, na2, ce, lanes), F32),
            pltpu.VMEM((2, na2, ce, lanes), F32),
            pltpu.VMEM((3, na2 + 2, ce, lanes), F32),
            pltpu.VMEM((na2, ce, lanes), F32),
            pltpu.VMEM((3, rows, lanes), F32),
            pltpu.VMEM((ca, cc, lanes), F32),
            pltpu.VMEM((ca, cc, lanes), F32),
            pltpu.VMEM((cm, cc, lanes), F32),
            pltpu.VMEM((cm, cc, lanes), F32),
            pltpu.VMEM((2, ca, lanes), F32),
            pltpu.VMEM((2, cm, lanes), F32),
            pltpu.VMEM((9, lanes, lanes), BF16),
            pltpu.VMEM((9, lanes, lanes), BF16),
            pltpu.VMEM((9, lanes, lanes), BF16),
            pltpu.VMEM((lanes, lanes), F32),
            pltpu.VMEM((8, 3 * ca, lanes), F32),
            pltpu.VMEM((8, 3 * ca, lanes), F32),
            pltpu.VMEM((8, rows1, lanes), F32),
            pltpu.VMEM((8, rows1, lanes), F32),
            pltpu.VMEM((2, 2, half, 8, lanes), F32),
            pltpu.VMEM((2, 2, half, 8, lanes), F32),
            pltpu.VMEM((2, 3, half, 8, lanes), F32),
            pltpu.VMEM((2, 3, half, 8, lanes), F32),
            pltpu.SemaphoreType.DMA((8, 4)),
            pltpu.SemaphoreType.DMA((8, 4)),
            pltpu.SemaphoreType.DMA((2, nax)),
            pltpu.SemaphoreType.DMA((2, nax)),
            pltpu.SemaphoreType.DMA((2, 2)),
            pltpu.SemaphoreType.DMA((2, 2)),
        ],
        compiler_params=pltpu.CompilerParams(
            collective_id=0, has_side_effects=True, vmem_limit_bytes=52 * 1024 * 1024
        ),
        name="vcycle",
    )(
        jnp.transpose(load, (0, 2, 1, 3)),
        region,
        family,
        stiffness,
        jnp.transpose(coupling, (1, 0, 2)),
        line_inverse.reshape(9, rr, rr),
        axial_inverse,
    )
    back = (0, 2, 1, 3)
    return jnp.transpose(sol, back), jnp.transpose(res, back), jnp.transpose(coarse, back)


def solution(mesh):
    field, cells = P("ax", "circ", None, None), P("ax", "circ", None)
    return jax.shard_map(
        body,
        mesh=mesh,
        in_specs=(field, cells, cells, P(), P(), P(), P()),
        out_specs=(field, field, field),
        check_vma=False,
    )
```

profile of v0, /device:TPU:0, one launch (start us, length us, event | category | flops | bytes accessed | tf_op | source)
XLA Modules:
  0.0 89.7 jit_solution(3912764166041267298)
XLA Ops:
  0.6 0.0 copy-start
  0.6 0.9 %copy-done = s32[8,32,192]{2,1,0:T(8,128)S(1)} copy-done((s32[8,32,192]{2,1,0:T(8,128)S(1)}, s32[8,32,192]{2,1,0:T(8,128)}, u32[]{:S(2)}) %copy-start) | copy-done | bytes 196632
  1.6 0.0 copy-start.1
  1.6 0.9 %copy-done.1 = s32[8,32,192]{2,1,0:T(8,128)S(1)} copy-done((s32[8,32,192]{2,1,0:T(8,128)S(1)}, s32[8,32,192]{2,1,0:T(8,128)}, u32[]{:S(2)}) %copy-start.1) | copy-done | bytes 196632
  2.5 0.0 copy-start.2
  2.5 0.7 copy-done.2
  3.2 0.0 copy-start.3
  3.2 0.7 copy-done.3
  3.9 0.0 copy-start.4
  3.9 0.7 copy-done.4
  4.6 82.1 %vcycle.1 = (f32[8,3,32,192]{3,2,1,0:T(8,128)S(1)}, f32[8,3,32,192]{3,2,1,0:T(8,128)}, f32[2,3,32,192]{3,2,1,0:T(8,128)S(1)}) custom-call(f32[8,3,32,192]{3,2,1,0:T(8,128)} %bitcast.11, s32[8,32,192]{2,1,0:T(8,128)S(1)} %copy-done, s32[8,32,192]{2,1,0:T(8,128)S(1)} %copy-done.1, f32[2,3]{1,0:T(2,128)S(1)} %copy-done.4, f32[3,2,3]{2,1,0:T(2,128)S(1)} %bitcast.8, ...), custom_call_target="tpu_custom_call" | custom-call | tf_op jit(solution)/shard_map/vcycle/pallas_call | solution.py:479
  86.7 0.0 copy-start.5
  86.7 0.9 copy.13
  87.6 0.5 copy-done.5
  88.2 0.9 copy.14
  89.0 0.7 copy.15
Async XLA Ops:
  0.6 1.0 %copy-start = (s32[8,32,192]{2,1,0:T(8,128)S(1)}, s32[8,32,192]{2,1,0:T(8,128)}, u32[]{:S(2)}) copy-start(s32[8,32,192]{2,1,0:T(8,128)} %region_ref.1) | copy-start | bytes 589828
  1.6 0.9 %copy-start.1 = (s32[8,32,192]{2,1,0:T(8,128)S(1)}, s32[8,32,192]{2,1,0:T(8,128)}, u32[]{:S(2)}) copy-start(s32[8,32,192]{2,1,0:T(8,128)} %family_ref.1) | copy-start | bytes 589828
  2.5 0.7 copy-start.2
  3.2 0.7 copy-start.3
  3.9 0.7 copy-start.4
  86.7 1.4 %copy-start.5 = (f32[8,3,32,192]{3,2,1,0:T(8,128)S(1)}, f32[8,3,32,192]{3,2,1,0:T(8,128)}, u32[]{:S(2)}) copy-start(f32[8,3,32,192]{3,2,1,0:T(8,128)} %get-tuple-element.7) | copy-start | bytes 1769476
where the time goes:
time: 90.1 us; the launch traced here: 89.7 us
  Pallas kernels  82.1 us (91%)
  local copies, waits for them, and re-layouts  6.91 us (8%)
    pallas_call x1, Pallas kernels, body(): pl.pallas_call(functools.partial(kernel, (nax, ncirc, ca, cc, rr, lanes))...  82.1 us
    unnamed x15, local copies, waits for them, and re-layouts  6.91 us

commit v1 on v0

--- a/solution.py
+++ b/solution.py
@@ -16,6 +16,16 @@
 
 def kernel(
     dims,
+    load_hbm,
+    region_hbm,
+    family_hbm,
+    stiff_hbm,
+    coup_hbm,
+    inv_hbm,
+    axial_hbm,
+    sol_ref,
+    res_ref,
+    coarse_ref,
     load_ref,
     region_ref,
     family_ref,
@@ -23,9 +33,7 @@
     coup_ref,
     inv_ref,
     axial_ref,
-    sol_ref,
-    res_ref,
-    coarse_ref,
+    in_sem,
     b0,
     u0a,
     u0b,
@@ -78,6 +86,23 @@
     c_left, c_right = lax.rem(me_c + ncirc - 1, ncirc), lax.rem(me_c + 1, ncirc)
     has_left, has_right = pos > 0, pos < nax - 1
 
+    arrivals = [
+        pltpu.make_async_copy(source, target, in_sem.at[i])
+        for i, (source, target) in enumerate(
+            (
+                (load_hbm, load_ref),
+                (region_hbm, region_ref),
+                (family_hbm, family_ref),
+                (stiff_hbm, stiff_ref),
+                (coup_hbm, coup_ref),
+                (inv_hbm, inv_ref),
+                (axial_hbm, axial_ref),
+            )
+        )
+    ]
+    for arrival in arrivals:
+        arrival.start()
+
     barrier = pltpu.get_barrier_semaphore()
     for d in range(1, nax):
         pl.semaphore_signal(barrier, inc=1, device_id=(lax.rem(pos + d, nax), me_c))
@@ -85,6 +110,7 @@
     pl.semaphore_signal(barrier, inc=1, device_id=(pos, c_right))
 
     b0[:, 1 : ca + 1, 0:cc, lanes - 128 : lanes] = jnp.zeros((3, ca, cc, 128), F32)
+    arrivals[0].wait()
     for k in range(3):
         b0[k, 1 : ca + 1, 0:cc, 0:rr] = load_ref[:, k]
 
@@ -180,28 +206,42 @@
             right.wait_send()
             left.wait_recv()
 
-    def gather_copies(which, buf):
-        pairs = []
-        for d in range(1, nax):
-            to, of = lax.rem(pos + d, nax), lax.rem(pos + nax - d, nax)
-            out = pltpu.make_async_remote_copy(
-                src_ref=buf.at[:, pl.ds(pos * cq, cq), 0:cc],
-                dst_ref=buf.at[:, pl.ds(pos * cq, cq), 0:cc],
-                send_sem=gsend.at[which, d],
-                recv_sem=grecv.at[which, d],
-                device_id=(to, me_c),
-            )
-            come = pltpu.make_async_remote_copy(
-                src_ref=buf.at[:, pl.ds(of * cq, cq), 0:cc],
-                dst_ref=buf.at[:, pl.ds(of * cq, cq), 0:cc],
-                send_sem=gsend.at[which, d],
-                recv_sem=grecv.at[which, d],
-                device_id=(to, me_c),
-            )
-            pairs.append((out, come))
-        return pairs
-
-    half = na2 // 2
+    mate = pos + 1 - 2 * lax.rem(pos, 2)
+
+    def block_copy(which, slot, buf, cols, block, to):
+        part = (slice(None), pl.ds(block * cq, cq), slice(*cols))
+        return pltpu.make_async_remote_copy(
+            src_ref=buf.at[part],
+            dst_ref=buf.at[part],
+            send_sem=gsend.at[which, slot],
+            recv_sem=grecv.at[which, slot],
+            device_id=(to, me_c),
+        )
+
+    def across(j):
+        return lax.rem(pos + 2 * j, nax), lax.rem(pos + nax - 2 * j, nax)
+
+    def gather_start(which, buf, cols):
+        for j in range(1, nax // 2):
+            block_copy(which, j, buf, cols, pos, across(j)[0]).start()
+        block_copy(which, 0, buf, cols, pos, mate).start()
+
+    def gather_forward(which, buf, cols):
+        for j in range(1, nax // 2):
+            block_copy(which, j, buf, cols, across(j)[1], across(j)[0]).wait_recv()
+            block_copy(which, nax // 2 + j, buf, cols, across(j)[1], mate).start()
+
+    def gather_finish(which, buf, cols):
+        for j in range(1, nax // 2):
+            block_copy(which, j, buf, cols, pos, across(j)[0]).wait_send()
+            block_copy(which, nax // 2 + j, buf, cols, across(j)[1], mate).wait_send()
+            theirs = lax.rem(mate + nax - 2 * j, nax)
+            block_copy(which, nax // 2 + j, buf, cols, theirs, mate).wait_recv()
+        block_copy(which, 0, buf, cols, pos, mate).wait_send()
+        block_copy(which, 0, buf, cols, mate, mate).wait_recv()
+
+    half = cq // 2
+    base = pos * cq
     low = lax.broadcasted_iota(jnp.int32, (8, lanes), 0) < DEEP
 
     def turn(tile):
@@ -222,9 +262,11 @@
     def deep_start(which, buf, fields, pack, got):
         for f in range(fields):
             for a in range(half):
-                pack[0, f, a] = jnp.where(low, buf[f, a, 0:8, :], turn(buf[f, a + half, 0:8, :]))
+                pack[0, f, a] = jnp.where(low, buf[f, base + a, 0:8, :], turn(buf[f, base + a + half, 0:8, :]))
                 pack[1, f, a] = jnp.where(
-                    low, turn(buf[f, a, cc - 8 : cc, :]), buf[f, a + half, cc - 8 : cc, :]
+                    low,
+                    turn(buf[f, base + a, cc - 8 : cc, :]),
+                    buf[f, base + a + half, cc - 8 : cc, :],
                 )
         for copy in deep_copies(which, pack, got):
             copy.start()
@@ -235,8 +277,8 @@
         for f in range(fields):
             for a in range(half):
                 right, left = got[0, f, a], got[1, f, a]
-                buf[f, a, cc:ce, :] = jnp.where(low, right, turn(left))
-                buf[f, a + half, cc:ce, :] = jnp.where(low, turn(right), left)
+                buf[f, base + a, cc:ce, :] = jnp.where(low, right, turn(left))
+                buf[f, base + a + half, cc:ce, :] = jnp.where(low, turn(right), left)
 
     def split(x):
         hi = x.astype(BF16)
@@ -251,6 +293,8 @@
         small = dot(lo, wh[i]) + dot(hi, wl[i]) + dot(mid, wm[i])
         return dot(hi, wh[i]) + (dot(mid, wh[i]) + dot(hi, wm[i]) + small)
 
+    arrivals[3].wait()
+    arrivals[4].wait()
     stiff = [[stiff_ref[s, k] for k in range(3)] for s in range(2)]
     first = [[coup_ref[k, 0, e] for e in range(3)] for k in range(3)]
     diff = [[coup_ref[k, 1, e] - first[k][e] for e in range(3)] for k in range(3)]
@@ -344,6 +388,8 @@
     edge_start(0, b0, ca, pack0, got0)
 
     zeros = jnp.zeros((ca, cc, lanes), F32)
+    arrivals[1].wait()
+    arrivals[2].wait()
     reg0[...] = zeros
     sh0[...] = zeros
     reg0[:, :, 0:rr] = jnp.where(region_ref[...] == 0, 0.0, 1.0)
@@ -353,13 +399,15 @@
             mid_c[a] = 0.5 * (fine_c[2 * a] + fine_c[2 * a + 1])
         for a in range(cq):
             c2[f, pos * cq + a, 0:cc, :] = 0.5 * (mid_c[2 * a] + mid_c[2 * a + 1])
-    for out, _ in gather_copies(0, c2):
-        out.start()
+    gather_start(0, c2, (0, cc))
+    deep_start(0, c2, 2, packc, gotc)
     for ends, reg, rows in ((ends0, reg0, ca), (ends1, reg1, cm)):
         for a in range(rows):
             ends[0, a : a + 1, :] = reg[a, cc - 1 : cc, :]
             ends[1, a : a + 1, :] = reg[a, 0:1, :]
 
+    arrivals[5].wait()
+    arrivals[6].wait()
     wtmp[...] = jnp.zeros((lanes, lanes), F32)
 
     def prepare(i, carry):
@@ -375,10 +423,10 @@
     correct(0, ca, u0a, u0b)
 
     def coefficients_on():
-        for out, come in gather_copies(0, c2):
-            out.wait_send()
-            come.wait_recv()
-        deep_start(0, c2, 2, packc, gotc)
+        deep_finish(0, c2, 2, packc, gotc)
+        gather_start(1, c2, (cc, ce))
+        gather_forward(0, c2, (0, cc))
+        gather_finish(0, c2, (0, cc))
 
     edge_remainder(1, u0b, 0, ca, b0, pack0.at[2:4], got0.at[2:4], True, coefficients_on)
 
@@ -397,14 +445,16 @@
 
     restrict_into(cm, into_b2)
 
-    for out, _ in gather_copies(1, b2):
-        out.start()
-    deep_finish(0, c2, 2, packc, gotc)
-    for out, come in gather_copies(1, b2):
-        out.wait_send()
-        come.wait_recv()
     deep_start(1, b2, 3, packb, gotb)
+    gather_start(2, b2, (0, cc))
+    gather_forward(1, c2, (cc, ce))
+    gather_finish(1, c2, (cc, ce))
+    gather_forward(2, b2, (0, cc))
     deep_finish(1, b2, 3, packb, gotb)
+    gather_start(3, b2, (cc, ce))
+    gather_forward(3, b2, (cc, ce))
+    gather_finish(2, b2, (0, cc))
+    gather_finish(3, b2, (cc, ce))
 
     def coarse_solve(first_time):
         def one(k, carry):
@@ -472,10 +522,10 @@
     rows = max(ca * cc, na2 * ce)
     rows1 = -(-3 * cm // 8) * 8
     vmem = pl.BlockSpec(memory_space=pltpu.VMEM)
-    smem = pl.BlockSpec(memory_space=pltpu.SMEM)
+    hbm = pl.BlockSpec(memory_space=pltpu.HBM)
     fine = pltpu.VMEM((3, ca + 2, ce, lanes), F32)
     mid = pltpu.VMEM((3, cm + 2, ce, lanes), F32)
-    half = na2 // 2
+    half = cq // 2
     sol, res, coarse = pl.pallas_call(
         functools.partial(kernel, (nax, ncirc, ca, cc, rr, lanes)),
         out_shape=[
@@ -483,9 +533,19 @@
             jax.ShapeDtypeStruct((ca, 3, cc, rr), F32),
             jax.ShapeDtypeStruct((cq, 3, cc, rr), F32),
         ],
-        in_specs=[vmem, vmem, vmem, smem, smem, vmem, smem],
+        in_specs=[hbm] * 7,
         out_specs=[vmem, vmem, vmem],
-        scratch_shapes=[fine] * 6
+        scratch_shapes=[
+            pltpu.VMEM((ca, 3, cc, rr), F32),
+            pltpu.VMEM((ca, cc, rr), jnp.int32),
+            pltpu.VMEM((ca, cc, rr), jnp.int32),
+            pltpu.SMEM((2, 3), F32),
+            pltpu.SMEM((3, 2, 3), F32),
+            pltpu.VMEM((9, rr, rr), F32),
+            pltpu.SMEM((na2, na2), F32),
+            pltpu.SemaphoreType.DMA((7,)),
+        ]
+        + [fine] * 6
         + [mid] * 6
         + [
             pltpu.VMEM((3, na2, ce, lanes), F32),
@@ -513,8 +573,8 @@
             pltpu.VMEM((2, 3, half, 8, lanes), F32),
             pltpu.SemaphoreType.DMA((8, 4)),
             pltpu.SemaphoreType.DMA((8, 4)),
-            pltpu.SemaphoreType.DMA((2, nax)),
-            pltpu.SemaphoreType.DMA((2, nax)),
+            pltpu.SemaphoreType.DMA((4, nax)),
+            pltpu.SemaphoreType.DMA((4, nax)),
             pltpu.SemaphoreType.DMA((2, 2)),
             pltpu.SemaphoreType.DMA((2, 2)),
         ],

time: 90.1 us -> 83.3 us (0.925)
  Pallas kernels: 82.1 us -> 75.4 us
    pallas_call x1, Pallas kernels: 82.1 us -> 75.4 us  [body(): pl.pallas_call(functools.partial(kernel, (nax, ncirc, ca, cc, rr, lanes))...]
where the time goes in v1:
time: 83.3 us; the launch traced here: 83 us
  Pallas kernels  75.4 us (91%)
  local copies, waits for them, and re-layouts  6.91 us (8%)
    pallas_call x1, Pallas kernels, body(): pl.pallas_call(functools.partial(kernel, (nax, ncirc, ca, cc, rr, lanes))...  75.4 us
    unnamed x15, local copies, waits for them, and re-layouts  6.91 us

profile of v1, /device:TPU:0, one launch (start us, length us, event | category | flops | bytes accessed | tf_op | source)
XLA Modules:
  0.0 83.0 jit_solution(1638727134824111856)
XLA Ops:
  0.6 0.0 copy-start
  0.6 0.9 %copy-done = s32[8,32,192]{2,1,0:T(8,128)S(1)} copy-done((s32[8,32,192]{2,1,0:T(8,128)S(1)}, s32[8,32,192]{2,1,0:T(8,128)}, u32[]{:S(2)}) %copy-start) | copy-done | bytes 196632
  1.6 0.0 copy-start.1
  1.6 0.9 %copy-done.1 = s32[8,32,192]{2,1,0:T(8,128)S(1)} copy-done((s32[8,32,192]{2,1,0:T(8,128)S(1)}, s32[8,32,192]{2,1,0:T(8,128)}, u32[]{:S(2)}) %copy-start.1) | copy-done | bytes 196632
  2.5 0.0 copy-start.2
  2.5 0.7 copy-done.2
  3.2 0.0 copy-start.3
  3.2 0.7 copy-done.3
  3.9 0.0 copy-start.4
  3.9 0.7 copy-done.4
  4.6 75.4 %vcycle.1 = (f32[8,3,32,192]{3,2,1,0:T(8,128)S(1)}, f32[8,3,32,192]{3,2,1,0:T(8,128)}, f32[2,3,32,192]{3,2,1,0:T(8,128)S(1)}) custom-call(f32[8,3,32,192]{3,2,1,0:T(8,128)} %bitcast.11, s32[8,32,192]{2,1,0:T(8,128)S(1)} %copy-done, s32[8,32,192]{2,1,0:T(8,128)S(1)} %copy-done.1, f32[2,3]{1,0:T(2,128)S(1)} %copy-done.4, f32[3,2,3]{2,1,0:T(2,128)S(1)} %bitcast.8, ...), custom_call_target="tpu_custom_call" | custom-call | tf_op jit(solution)/shard_map/vcycle/pallas_call | solution.py:529
  80.0 0.0 copy-start.5
  80.0 0.9 %copy.13 = f32[8,32,3,192]{3,1,2,0:T(8,128)} copy(f32[8,32,3,192]{3,1,2,0:T(8,128)S(1)} %bitcast.6) | data formatting | bytes 1179648
  80.9 0.5 copy-done.5
  81.4 0.9 %copy.14 = f32[8,32,3,192]{3,1,2,0:T(8,128)} copy(f32[8,32,3,192]{3,1,2,0:T(8,128)S(1)} %bitcast.10) | data formatting | bytes 1179648
  82.3 0.7 copy.15
Async XLA Ops:
  0.6 1.0 %copy-start = (s32[8,32,192]{2,1,0:T(8,128)S(1)}, s32[8,32,192]{2,1,0:T(8,128)}, u32[]{:S(2)}) copy-start(s32[8,32,192]{2,1,0:T(8,128)} %region_hbm.1) | copy-start | bytes 589828
  1.6 0.9 %copy-start.1 = (s32[8,32,192]{2,1,0:T(8,128)S(1)}, s32[8,32,192]{2,1,0:T(8,128)}, u32[]{:S(2)}) copy-start(s32[8,32,192]{2,1,0:T(8,128)} %family_hbm.1) | copy-start | bytes 589828
  2.5 0.7 copy-start.2
  3.2 0.7 copy-start.3
  3.9 0.7 copy-start.4
  80.0 1.4 %copy-start.5 = (f32[8,3,32,192]{3,2,1,0:T(8,128)S(1)}, f32[8,3,32,192]{3,2,1,0:T(8,128)}, u32[]{:S(2)}) copy-start(f32[8,3,32,192]{3,2,1,0:T(8,128)} %get-tuple-element.7) | copy-start | bytes 1769476

commit v2 on v1

--- a/solution.py
+++ b/solution.py
@@ -23,6 +23,9 @@
     coup_hbm,
     inv_hbm,
     axial_hbm,
+    sol_hbm,
+    res_hbm,
+    coarse_hbm,
     sol_ref,
     res_ref,
     coarse_ref,
@@ -34,6 +37,7 @@
     inv_ref,
     axial_ref,
     in_sem,
+    out_sem,
     b0,
     u0a,
     u0b,
@@ -103,6 +107,13 @@
     for arrival in arrivals:
         arrival.start()
 
+    departures = [
+        pltpu.make_async_copy(source, target, out_sem.at[i])
+        for i, (source, target) in enumerate(
+            ((sol_ref, sol_hbm), (res_ref, res_hbm), (coarse_ref, coarse_hbm))
+        )
+    ]
+
     barrier = pltpu.get_barrier_semaphore()
     for d in range(1, nax):
         pl.semaphore_signal(barrier, inc=1, device_id=(lax.rem(pos + d, nax), me_c))
@@ -139,43 +150,27 @@
     zero_row(u2, 0)
     zero_row(u2, na2 + 1)
 
-    def edge_copies(x, buf, rows, pack, got):
-        left = pltpu.make_async_remote_copy(
-            src_ref=buf.at[:, 1, 0:cc],
-            dst_ref=buf.at[:, rows + 1, 0:cc],
-            send_sem=send_sem.at[x, 0],
-            recv_sem=recv_sem.at[x, 1],
-            device_id=(ax_left, me_c),
-        )
-        right = pltpu.make_async_remote_copy(
-            src_ref=buf.at[:, rows, 0:cc],
-            dst_ref=buf.at[:, 0, 0:cc],
-            send_sem=send_sem.at[x, 1],
-            recv_sem=recv_sem.at[x, 0],
-            device_id=(ax_right, me_c),
-        )
-        down = pltpu.make_async_remote_copy(
-            src_ref=pack.at[0],
-            dst_ref=got.at[0],
-            send_sem=send_sem.at[x, 2],
-            recv_sem=recv_sem.at[x, 2],
-            device_id=(pos, c_left),
-        )
-        up = pltpu.make_async_remote_copy(
-            src_ref=pack.at[1],
-            dst_ref=got.at[1],
-            send_sem=send_sem.at[x, 3],
-            recv_sem=recv_sem.at[x, 3],
-            device_id=(pos, c_right),
-        )
+    def edge_copies(x, buf, rows, pack, got, k):
+        def copy(source, target, sent, landed, to):
+            return pltpu.make_async_remote_copy(
+                src_ref=source,
+                dst_ref=target,
+                send_sem=send_sem.at[x, sent, k],
+                recv_sem=recv_sem.at[x, landed, k],
+                device_id=to,
+            )
+
+        left = copy(buf.at[k, 1, 0:cc], buf.at[k, rows + 1, 0:cc], 0, 1, (ax_left, me_c))
+        right = copy(buf.at[k, rows, 0:cc], buf.at[k, 0, 0:cc], 1, 0, (ax_right, me_c))
+        down = copy(pack.at[0, k], got.at[0, k], 2, 2, (pos, c_left))
+        up = copy(pack.at[1, k], got.at[1, k], 3, 3, (pos, c_right))
         return left, right, down, up
 
-    def edge_start(x, buf, rows, pack, got):
-        left, right, down, up = edge_copies(x, buf, rows, pack, got)
-        for k in range(3):
-            for a in range(rows):
-                pack[0, k * rows + a : k * rows + a + 1, :] = buf[k, a + 1, 0:1, :]
-                pack[1, k * rows + a : k * rows + a + 1, :] = buf[k, a + 1, cc - 1 : cc, :]
+    def edge_send(x, buf, rows, pack, got, k):
+        left, right, down, up = edge_copies(x, buf, rows, pack, got, k)
+        for a in range(rows):
+            pack[0, k, a : a + 1, :] = buf[k, a + 1, 0:1, :]
+            pack[1, k, a : a + 1, :] = buf[k, a + 1, cc - 1 : cc, :]
         down.start()
         up.start()
 
@@ -188,23 +183,23 @@
             right.start()
 
     def edge_finish(x, buf, rows, pack, got, keep=False):
-        left, right, down, up = edge_copies(x, buf, rows, pack, got)
-        down.wait()
-        up.wait()
-        for k in range(3 if keep else 0):
-            for a in range(rows):
-                buf[k, a + 1, cc : cc + 1, :] = got[0, k * rows + a : k * rows + a + 1, :]
-                buf[k, a + 1, ce - 1 : ce, :] = got[1, k * rows + a : k * rows + a + 1, :]
-
-        @pl.when(has_left)
-        def _():
-            left.wait_send()
-            right.wait_recv()
-
-        @pl.when(has_right)
-        def _():
-            right.wait_send()
-            left.wait_recv()
+        for k in range(3):
+            left, right, down, up = edge_copies(x, buf, rows, pack, got, k)
+            down.wait()
+            up.wait()
+            for a in range(rows if keep else 0):
+                buf[k, a + 1, cc : cc + 1, :] = got[0, k, a : a + 1, :]
+                buf[k, a + 1, ce - 1 : ce, :] = got[1, k, a : a + 1, :]
+
+            @pl.when(has_left)
+            def _():
+                left.wait_send()
+                right.wait_recv()
+
+            @pl.when(has_right)
+            def _():
+                right.wait_send()
+                left.wait_recv()
 
     mate = pos + 1 - 2 * lax.rem(pos, 2)
 
@@ -338,27 +333,32 @@
     def whole_remainder(u, level, rows, rhs):
         remainder(u, level, 0, rows, 1, cc, rhs, 1, False)
 
+    def side_columns(level, rows, changes):
+        ends = edges[level]
+        for k in range(3):
+            for side, col in ((0, cc - 1), (1, 0)):
+                coef = stiff[0][k] + ends[side, 0:rows, :] * (stiff[1][k] - stiff[0][k])
+                parts = [(got[side, k] - pack[side, k], times) for pack, got, times in changes]
+                for a in range(rows):
+                    place = a * cc + col
+                    more = sum(part[a // times : a // times + 1] for part, times in parts)
+                    rbuf[k, place : place + 1, :] = (
+                        rbuf[k, place : place + 1, :] + coef[a : a + 1] * more
+                    )
+
     def edge_remainder(x, u, level, rows, rhs, pack, got, keep=False, between=None):
-        edge_start(x, u, rows, pack, got)
         remainder(u, level, 1, rows - 2, 1, cc, rhs, 1, True)
         if between is not None:
             between()
         edge_finish(x, u, rows, pack, got, keep)
         remainder(u, level, 0, 2, rows - 1, cc, rhs, 1, True)
-        ends = edges[level]
-        for k in range(3):
-            at = k * rows
-            for side, col in ((0, cc - 1), (1, 0)):
-                coef = stiff[0][k] + ends[side, 0:rows, :] * (stiff[1][k] - stiff[0][k])
-                more = coef * (got[side, at : at + rows, :] - pack[side, at : at + rows, :])
-                for a in range(rows):
-                    place = a * cc + col
-                    rbuf[k, place : place + 1, :] = rbuf[k, place : place + 1, :] + more[a : a + 1]
-
-    def correct(level, rows, old, new):
+        side_columns(level, rows, [(pack, got, 1)])
+
+    def correct(level, rows, old, new, x, pack, got):
         def one(k, carry):
             step = line(level, k, rbuf[k, 0 : rows * cc, :]).reshape(rows, cc, lanes)
             new[k, 1 : rows + 1, 0:cc, :] = old[k, 1 : rows + 1, 0:cc, :] + step
+            edge_send(x, new, rows, pack, got, k)
             return carry
 
         lax.fori_loop(0, 3, one, 0)
@@ -371,10 +371,11 @@
 
         lax.fori_loop(0, 3, one, 0)
 
-    def start_from(level, rhs, rows, new):
+    def start_from(level, rhs, rows, new, x, pack, got):
         def one(k, carry):
             step = line(level, k, rhs[k, 1 : rows + 1, 0:cc, :].reshape(rows * cc, lanes))
             new[k, 1 : rows + 1, 0:cc, :] = step.reshape(rows, cc, lanes)
+            edge_send(x, new, rows, pack, got, k)
             return carry
 
         lax.fori_loop(0, 3, one, 0)
@@ -385,7 +386,8 @@
             write(k, 0.5 * (r[:, 0] + r[:, 1]))
 
     pl.semaphore_wait(barrier, nax + 1)
-    edge_start(0, b0, ca, pack0, got0)
+    for k in range(3):
+        edge_send(0, b0, ca, pack0, got0, k)
 
     zeros = jnp.zeros((ca, cc, lanes), F32)
     arrivals[1].wait()
@@ -420,7 +422,7 @@
     edge_finish(0, b0, ca, pack0, got0, True)
     first_sweep(0, b0, ca + 2, u0a)
     whole_remainder(u0a, 0, ca, b0)
-    correct(0, ca, u0a, u0b)
+    correct(0, ca, u0a, u0b, 1, pack0.at[2:4], got0.at[2:4])
 
     def coefficients_on():
         deep_finish(0, c2, 2, packc, gotc)
@@ -428,16 +430,16 @@
         gather_forward(0, c2, (0, cc))
         gather_finish(0, c2, (0, cc))
 
-    edge_remainder(1, u0b, 0, ca, b0, pack0.at[2:4], got0.at[2:4], True, coefficients_on)
+    edge_remainder(1, u0b, 0, ca, b0, pack0.at[2:4], got0.at[2:4], False, coefficients_on)
 
     def into_b1(k, value):
         b1[k, 1 : cm + 1, 0:cc, :] = value
 
     restrict_into(ca, into_b1)
 
-    start_from(1, b1, cm, u1a)
+    start_from(1, b1, cm, u1a, 2, pack1, got1)
     edge_remainder(2, u1a, 1, cm, b1, pack1, got1)
-    correct(1, cm, u1a, u1b)
+    correct(1, cm, u1a, u1b, 3, pack1.at[2:4], got1.at[2:4])
     edge_remainder(3, u1b, 1, cm, b1, pack1.at[2:4], got1.at[2:4], True)
 
     def into_b2(k, value):
@@ -484,32 +486,47 @@
     for a in range(cq):
         for k in range(3):
             coarse_ref[a, k] = u2[k, pos * cq + a + 1, 0:cc, 0:rr]
+    departures[2].start()
 
     for i in range(cm + 2):
         for k in range(3):
             u1c[k, i] = u1b[k, i] + u2[k, pos * cq + (i + 1) // 2]
     whole_remainder(u1c, 1, cm, b1)
-    correct(1, cm, u1c, u1d)
+    correct(1, cm, u1c, u1d, 4, pack1.at[4:6], got1.at[4:6])
     edge_remainder(4, u1d, 1, cm, b1, pack1.at[4:6], got1.at[4:6])
-    correct(1, cm, u1d, u1e)
-    edge_start(5, u1e, cm, pack1.at[6:8], got1.at[6:8])
-    edge_finish(5, u1e, cm, pack1.at[6:8], got1.at[6:8], True)
-
-    for i in range(ca + 2):
+    correct(1, cm, u1d, u1e, 5, pack1.at[6:8], got1.at[6:8])
+
+    def lift(i):
         for k in range(3):
-            u0c[k, i] = u0b[k, i] + u1e[k, (i + 1) // 2]
-    whole_remainder(u0c, 0, ca, b0)
-    correct(0, ca, u0c, u0d)
+            u0c[k, i, 0:cc, :] = u0b[k, i, 0:cc, :] + u1e[k, (i + 1) // 2, 0:cc, :]
+
+    for i in range(1, ca + 1):
+        lift(i)
+    remainder(u0c, 0, 1, ca - 2, 1, cc, b0, 1, True)
+    edge_finish(5, u1e, cm, pack1.at[6:8], got1.at[6:8])
+    lift(0)
+    lift(ca + 1)
+    remainder(u0c, 0, 0, 2, ca - 1, cc, b0, 1, True)
+    side_columns(
+        0,
+        ca,
+        [(pack0.at[2:4], got0.at[2:4], 1), (pack1.at[6:8], got1.at[6:8], 2)],
+    )
+    correct(0, ca, u0c, u0d, 6, pack0.at[4:6], got0.at[4:6])
     edge_remainder(6, u0d, 0, ca, b0, pack0.at[4:6], got0.at[4:6])
-    correct(0, ca, u0d, u0e)
+    correct(0, ca, u0d, u0e, 7, pack0.at[6:8], got0.at[6:8])
 
     def solution_out():
         for k in range(3):
             sol_ref[:, k] = u0e[k, 1 : ca + 1, 0:cc, 0:rr]
+        departures[0].start()
 
     edge_remainder(7, u0e, 0, ca, b0, pack0.at[6:8], got0.at[6:8], False, solution_out)
     for k in range(3):
         res_ref[:, k] = rbuf[k, 0 : ca * cc, 0:rr].reshape(ca, cc, rr)
+    departures[1].start()
+    for departure in departures:
+        departure.wait()
 
 
 def body(load, region, family, stiffness, coupling, line_inverse, axial_inverse):
@@ -520,8 +537,6 @@
     cm, cq = ca // 2, ca // 4
     na2 = cq * nax
     rows = max(ca * cc, na2 * ce)
-    rows1 = -(-3 * cm // 8) * 8
-    vmem = pl.BlockSpec(memory_space=pltpu.VMEM)
     hbm = pl.BlockSpec(memory_space=pltpu.HBM)
     fine = pltpu.VMEM((3, ca + 2, ce, lanes), F32)
     mid = pltpu.VMEM((3, cm + 2, ce, lanes), F32)
@@ -534,8 +549,11 @@
             jax.ShapeDtypeStruct((cq, 3, cc, rr), F32),
         ],
         in_specs=[hbm] * 7,
-        out_specs=[vmem, vmem, vmem],
+        out_specs=[hbm] * 3,
         scratch_shapes=[
+            pltpu.VMEM((ca, 3, cc, rr), F32),
+            pltpu.VMEM((ca, 3, cc, rr), F32),
+            pltpu.VMEM((cq, 3, cc, rr), F32),
             pltpu.VMEM((ca, 3, cc, rr), F32),
             pltpu.VMEM((ca, cc, rr), jnp.int32),
             pltpu.VMEM((ca, cc, rr), jnp.int32),
@@ -544,6 +562,7 @@
             pltpu.VMEM((9, rr, rr), F32),
             pltpu.SMEM((na2, na2), F32),
             pltpu.SemaphoreType.DMA((7,)),
+            pltpu.SemaphoreType.DMA((3,)),
         ]
         + [fine] * 6
         + [mid] * 6
@@ -563,23 +582,23 @@
             pltpu.VMEM((9, lanes, lanes), BF16),
             pltpu.VMEM((9, lanes, lanes), BF16),
             pltpu.VMEM((lanes, lanes), F32),
-            pltpu.VMEM((8, 3 * ca, lanes), F32),
-            pltpu.VMEM((8, 3 * ca, lanes), F32),
-            pltpu.VMEM((8, rows1, lanes), F32),
-            pltpu.VMEM((8, rows1, lanes), F32),
+            pltpu.VMEM((8, 3, ca, lanes), F32),
+            pltpu.VMEM((8, 3, ca, lanes), F32),
+            pltpu.VMEM((8, 3, cm, lanes), F32),
+            pltpu.VMEM((8, 3, cm, lanes), F32),
             pltpu.VMEM((2, 2, half, 8, lanes), F32),
             pltpu.VMEM((2, 2, half, 8, lanes), F32),
             pltpu.VMEM((2, 3, half, 8, lanes), F32),
             pltpu.VMEM((2, 3, half, 8, lanes), F32),
-            pltpu.SemaphoreType.DMA((8, 4)),
-            pltpu.SemaphoreType.DMA((8, 4)),
+            pltpu.SemaphoreType.DMA((8, 4, 3)),
+            pltpu.SemaphoreType.DMA((8, 4, 3)),
             pltpu.SemaphoreType.DMA((4, nax)),
             pltpu.SemaphoreType.DMA((4, nax)),
             pltpu.SemaphoreType.DMA((2, 2)),
             pltpu.SemaphoreType.DMA((2, 2)),
         ],
         compiler_params=pltpu.CompilerParams(
-            collective_id=0, has_side_effects=True, vmem_limit_bytes=52 * 1024 * 1024
+            collective_id=0, has_side_effects=True, vmem_limit_bytes=63 * 1024 * 1024
         ),
         name="vcycle",
     )(

time: 83.3 us -> 79.3 us (0.952)
  local copies, waits for them, and re-layouts: 6.91 us -> 3.74 us
    unnamed x15 -> x7, local copies, waits for them, and re-layouts: 6.91 us -> 3.74 us
where the time goes in v2:
time: 79.3 us; the launch traced here: 79.1 us
  Pallas kernels  74.7 us (94%)
  local copies, waits for them, and re-layouts  3.74 us (5%)
    pallas_call x1, Pallas kernels, body(): pl.pallas_call(functools.partial(kernel, (nax, ncirc, ca, cc, rr, lanes))...  74.7 us
    unnamed x7, local copies, waits for them, and re-layouts  3.74 us

profile of v2, /device:TPU:0, one launch (start us, length us, event | category | flops | bytes accessed | tf_op | source)
XLA Modules:
  0.0 79.1 jit_solution(4062938845573929525)
XLA Ops:
  0.6 74.7 %vcycle.1 = (f32[8,3,32,192]{3,2,1,0:T(8,128)}, f32[8,3,32,192]{3,2,1,0:T(8,128)}, f32[2,3,32,192]{3,2,1,0:T(8,128)}) custom-call(f32[8,3,32,192]{3,2,1,0:T(8,128)} %bitcast.9, s32[8,32,192]{2,1,0:T(8,128)} %region_hbm.1, s32[8,32,192]{2,1,0:T(8,128)} %family_hbm.1, f32[2,3]{1,0:T(2,128)} %stiff_hbm.1, f32[3,2,3]{2,1,0:T(2,128)} %bitcast.11, ...), custom_call_target="tpu_custom_call" | custom-call | tf_op jit(solution)/shard_map/vcycle/pallas_call | solution.py:544
  75.4 0.0 copy-start
  75.4 0.0 copy-start.1
  75.4 2.2 %copy.13 = f32[8,32,3,192]{3,1,2,0:T(8,128)} copy(f32[8,32,3,192]{3,1,2,0:T(8,128)} %bitcast.8) | data formatting | bytes 1179648
  77.6 0.0 copy-done
  77.6 0.9 %copy.14 = f32[8,32,3,192]{3,1,2,0:T(8,128)} copy(f32[8,32,3,192]{3,1,2,0:T(8,128)S(1)} %bitcast.7) | data formatting | bytes 1179648
  78.4 0.0 copy-done.1
  78.4 0.7 copy.15
Async XLA Ops:
  75.4 2.2 %copy-start = (f32[8,3,32,192]{3,2,1,0:T(8,128)S(1)}, f32[8,3,32,192]{3,2,1,0:T(8,128)}, u32[]{:S(2)}) copy-start(f32[8,3,32,192]{3,2,1,0:T(8,128)} %get-tuple-element.7) | copy-start | bytes 1769476
  75.4 3.1 %copy-start.1 = (f32[2,3,32,192]{3,2,1,0:T(8,128)S(1)}, f32[2,3,32,192]{3,2,1,0:T(8,128)}, u32[]{:S(2)}) copy-start(f32[2,3,32,192]{3,2,1,0:T(8,128)} %get-tuple-element.8) | copy-start | bytes 442372
